TPU v7x, 32 devices: a whole 2x2x4 slice. The times are simulated.
32 devices in a mesh: ctx: 8 (over y, x, core), head: 4 (over z).
Axes of the slice: x: 2, y: 2, z: 4, core: 2. Of those that a mesh axis runs over, the one named last changes fastest.
Arguments:
- queries: bfloat16 [2048, 2048], P('ctx', 'head'), may hold values from -6 to 6
- keys: bfloat16 [2048, 2, 2048], P('ctx', None, 'head'), may hold values from -6 to 6
- values: bfloat16 [2048, 2, 2048], P('ctx', None, 'head'), may hold values from -6 to 6
- beta: float32 [16, 2, 2048], P('head', None, 'ctx'), as said below
- log_gate: float32 [16, 2048], P('head', 'ctx'), as said below
- norm_gain: float32 [2048], P('head'), may hold values from 0.1 to 1.9
- out_weight: bfloat16 [2048, 4096], P('head'), may hold values from -0.125 to 0.125
Outputs:
- mixed: bfloat16 [2048, 4096], P(('ctx', 'head'))
Inputs may be any that keep to these rules, and one draw needn't show every extreme that they name: `beta`: strictly below 2. `log_gate`: never positive.
All inputs are finite; a program needn't handle non-finite values.
Results may differ from a plain program's by a relative error of at most 0.025.
Values may be sent and summed in bfloat16 or wider, within the bound.
A program may use at most 128 MiB of HBM per device.

v0:
```python
import jax
import jax.numpy as jnp
from jax import lax
from jax.sharding import PartitionSpec as P

DH = 128
CT = 32


highest = lax.Precision.HIGHEST


def shifted(block, axis, distance):
    devices = range(lax.axis_size(axis))
    route = [(i - distance, i) for i in devices if i - distance in devices]
    return lax.ppermute(block, axis, route)


def normalize(key_rows):
    return key_rows * lax.rsqrt(jnp.sum(key_rows * key_rows, axis=-1, keepdims=True) + 1e-06)


def span_terms(query_rows, key_rows, value_rows, beta_values_rows, gate_rows):
    step_count = key_rows.shape[-2]
    cumulative = jnp.cumsum(gate_rows, axis=-1)
    later_step = jnp.arange(step_count)[:, None]
    earlier_step = jnp.arange(step_count)[None, :]
    strict = later_step > earlier_step
    gap_logs = cumulative[..., :, None] - cumulative[..., None, :]
    decay_ratio = jnp.where(strict, jnp.exp(jnp.where(strict, gap_logs, 0.0)), 0.0)
    key_inner = jnp.einsum("...sd,...rd->...sr", key_rows, key_rows, precision=highest)
    lower_part = decay_ratio * beta_values_rows[..., None, :] * key_inner
    system = jnp.eye(step_count, dtype=key_rows.dtype) + lower_part
    right_side = jnp.concatenate([value_rows, jnp.exp(cumulative)[..., None] * key_rows], axis=-1)
    solved = lax.linalg.triangular_solve(
        system, right_side, left_side=True, lower=True, unit_diagonal=True
    )
    value_width = value_rows.shape[-1]
    fresh_values = solved[..., :value_width]
    carried = solved[..., value_width:]
    span_total = cumulative[..., -1]
    scaled = (jnp.exp(span_total[..., None] - cumulative) * beta_values_rows)[..., None] * key_rows
    identity_key = jnp.eye(key_rows.shape[-1], dtype=key_rows.dtype)
    transition = jnp.exp(span_total)[..., None, None] * identity_key - jnp.einsum(
        "...rd,...re->...de", scaled, carried, precision=highest
    )
    offset = jnp.einsum("...rd,...re->...de", scaled, fresh_values, precision=highest)
    read_logs = cumulative[..., 1::2]
    row_index = jnp.arange(query_rows.shape[-2])[:, None]
    visible = 2 * row_index + 1 >= earlier_step
    read_gaps = read_logs[..., :, None] - cumulative[..., None, :]
    weight = jnp.where(visible, jnp.exp(jnp.where(visible, read_gaps, 0.0)), 0.0)
    scores = (
        jnp.einsum("...td,...rd->...tr", query_rows, key_rows, precision=highest)
        * weight
        * beta_values_rows[..., None, :]
    )
    lead_rows = jnp.exp(read_logs)[..., None] * query_rows - jnp.einsum(
        "...tr,...re->...te", scores, carried, precision=highest
    )
    local_part = jnp.einsum("...tr,...re->...te", scores, fresh_values, precision=highest)
    return (transition, offset, lead_rows, local_part)


def combine_maps(earlier, later):
    first_map, first_offset = earlier
    second_map, second_offset = later
    joined = jnp.einsum("...ij,...jk->...ik", second_map, first_map, precision=highest)
    moved = (
        jnp.einsum("...ij,...jk->...ik", second_map, first_offset, precision=highest)
        + second_offset
    )
    return (joined, moved)


def on_device(queries, keys, values, beta, log_gate, norm_gain, out_weight):
    head_count = beta.shape[0]
    token_count = queries.shape[0]
    spans = token_count // CT
    query_rows = jnp.transpose(queries.reshape(spans, CT, head_count, DH), (2, 0, 1, 3)).astype(
        jnp.float32
    )
    key_block = jnp.transpose(keys.reshape(spans, CT, 2, head_count, DH), (3, 0, 1, 2, 4))
    key_rows = normalize(key_block.reshape(head_count, spans, 2 * CT, DH).astype(jnp.float32))
    value_block = jnp.transpose(values.reshape(spans, CT, 2, head_count, DH), (3, 0, 1, 2, 4))
    value_rows = value_block.reshape(head_count, spans, 2 * CT, DH).astype(jnp.float32)
    beta_values_rows = jnp.transpose(beta, (0, 2, 1)).reshape(head_count, spans, 2 * CT)
    gate_rows = jnp.stack([log_gate, jnp.zeros_like(log_gate)], axis=-1).reshape(
        head_count, spans, 2 * CT
    )
    transition, offset, lead_rows, local_part = span_terms(
        query_rows, key_rows, value_rows, beta_values_rows, gate_rows
    )
    inclusive = lax.associative_scan(combine_maps, (transition, offset), axis=1)
    identity_map = jnp.broadcast_to(jnp.eye(DH, dtype=jnp.float32), (head_count, 1, DH, DH))
    before_map = jnp.concatenate([identity_map, inclusive[0][:, :-1]], axis=1)
    before_offset = jnp.concatenate(
        [jnp.zeros((head_count, 1, DH, DH), jnp.float32), inclusive[1][:, :-1]], axis=1
    )
    device_map = inclusive[0][:, -1]
    device_offset = inclusive[1][:, -1]

    def relay_state(turn_index, incoming):
        leaving = (
            jnp.einsum("hij,hjk->hik", device_map, incoming, precision=highest) + device_offset
        )
        return shifted(leaving.astype(jnp.bfloat16), "ctx", 1).astype(leaving.dtype)

    incoming = lax.fori_loop(
        0, lax.axis_size("ctx") - 1, relay_state, jnp.zeros((head_count, DH, DH), jnp.float32)
    )
    span_start = (
        jnp.einsum("hcij,hjk->hcik", before_map, incoming, precision=highest) + before_offset
    )
    read_rows = jnp.einsum("hctd,hcde->hcte", lead_rows, span_start, precision=highest) + local_part
    row_scale = lax.rsqrt(jnp.mean(read_rows * read_rows, axis=-1, keepdims=True) + 1e-06)
    normed = (read_rows * row_scale * norm_gain.reshape(head_count, 1, 1, DH)).astype(jnp.bfloat16)
    flat_rows = jnp.transpose(normed, (1, 2, 0, 3)).reshape(token_count, head_count * DH)
    return lax.psum_scatter(
        jnp.dot(flat_rows, out_weight, preferred_element_type=jnp.float32).astype(jnp.bfloat16),
        "head",
        scatter_dimension=0,
        tiled=True,
    )


def solution(mesh):
    return jax.shard_map(
        on_device,
        mesh=mesh,
        in_specs=(
            P("ctx", "head"),
            P("ctx", None, "head"),
            P("ctx", None, "head"),
            P("head", None, "ctx"),
            P("head", "ctx"),
            P("head"),
            P("head", None),
        ),
        out_specs=P(("ctx", "head"), None),
        check_vma=False,
    )
```

profile of v0, /device:TPU:0, one launch (start us, length us, event | category | flops | bytes accessed | tf_op | source)
XLA Modules:
  0.0 411.8 jit_solution(16377159715568255965)
XLA Ops:
  7.8 0.8 copy.54
  8.8 0.9 reduce_window_sum.11
  11.3 0.9 copy.43
  12.5 1.5 reshape.133
  15.0 1.1 convert_multiply_fusion
  16.2 2.2 mul.123
  18.4 1.5 reduce_sum.18
  19.9 1.1 add_rsqrt_fusion
  21.9 3.0 fusion.19
  24.9 158.1 %custom-call.3 = f32[4,8,1,64,64]{3,4,2,1,0:T(8,128)} custom-call(f32[4,8,1,64,64]{4,3,2,1,0:T(8,128)S(1)} %fusion.19), custom_call_target="InvertDiagBlocksLowerTriangular" | custom-call | tf_op jit(solution)/shard_map/triangular_solve | solution.py:35
  184.3 2.0 fusion.5
  186.3 5.4 %fusion.29 = f32[4,8,128,128]{3,2,1,0:T(8,128)} fusion(f32[4,8,64,256]{3,2,1,0:T(8,128)S(1)} %fusion.5, f32[4,8,64,128]{3,2,1,0:T(8,128)S(1)} %bitcast.94, f32[4,8,64]{2,1,0:T(8,128)S(1)} %get-tuple-element.51, f32[4,8,64]{2,1,0:T(8,128)S(1)} %copy.42), kind=kOutput, calls=%fused_computation.46 | convolution fusion | flops 403177472 | bytes 4227072 | tf_op jit(solution)/shard_map/...rd,...re->...de/dot_general | solution.py:47
  191.8 4.3 %multiply_subtract_fusion = f32[4,8,128,128]{3,2,1,0:T(8,128)S(1)} fusion(f32[128,128]{1,0:T(8,128)S(1)} %fusion.76, f32[4,8]{1,0:T(4,128)S(1)} %copy-done.31, f32[4,8,64,256]{3,2,1,0:T(8,128)S(1)} %fusion.5, f32[4,8,64,128]{3,2,1,0:T(8,128)S(1)} %bitcast.95, f32[4,8,64]{2,1,0:T(8,128)S(1)} %get-tuple-element.51, f32[4,8,64]{2,1,0:T(8,128)S(1)} %copy.42), kind=kOutput, calls=%fused_computation.18 | convolution fusion | flops 404226048 | bytes 4294656 | tf_op jit(solution)/shard_map/...rd,...re->...de/dot_general | solution.py:44
  196.1 1.1 fusion.26
  197.3 0.9 fusion.53
  199.0 0.9 pad_add_fusion.1
  199.9 0.8 pad_maximum_fusion.2
  200.7 5.8 %pad.42 = f32[4,4,128,128]{3,2,1,0:T(8,128)} pad(f32[4,2,128,128]{3,2,1,0:T(8,128)} %pad_maximum_fusion.2, f32[]{:T(128)} %constant.8.clone.1), padding=0_0_0x0_1_1x0_0_0x0_0_0 | pad | bytes 1572868 | tf_op jit(solution)/shard_map/pad | solution.py:94
  206.5 5.8 %pad.43 = f32[4,4,128,128]{3,2,1,0:T(8,128)} pad(f32[4,2,128,128]{3,2,1,0:T(8,128)} %pad_add_fusion.1, f32[]{:T(128)} %constant.8.clone.1), padding=0_0_0x1_0_1x0_0_0x0_0_0 | pad | bytes 1572868 | tf_op jit(solution)/shard_map/pad | solution.py:94
  212.3 3.3 fusion.44
  215.6 1.1 add.140
  216.7 0.8 copy-done.8
  217.6 1.2 convolution_add_fusion.1
  220.3 0.8 pad_add_fusion
  221.1 0.8 pad_maximum_fusion.3
  222.0 5.7 %pad.48 = f32[4,4,128,128]{3,2,1,0:T(8,128)} pad(f32[4,2,128,128]{3,2,1,0:T(8,128)} %pad_maximum_fusion.3, f32[]{:T(128)} %constant.8.clone.1), padding=0_0_0x0_1_1x0_0_0x0_0_0 | pad | bytes 1572868 | tf_op jit(solution)/shard_map/pad | solution.py:94
  227.7 5.8 %pad.49 = f32[4,4,128,128]{3,2,1,0:T(8,128)} pad(f32[4,2,128,128]{3,2,1,0:T(8,128)} %pad_add_fusion, f32[]{:T(128)} %constant.8.clone.1), padding=0_0_0x1_0_1x0_0_0x0_0_0 | pad | bytes 1572868 | tf_op jit(solution)/shard_map/pad | solution.py:94
  233.5 2.7 convolution_add_fusion.2
  236.2 1.1 add.147
  237.4 6.3 %pad.68 = f32[4,7,128,128]{3,2,1,0:T(8,128)} pad(f32[4,4,128,128]{3,2,1,0:T(8,128)S(1)} %pad_maximum_fusion.1, f32[]{:T(128)} %constant.8.clone.1), padding=0_0_0x0_0_1x0_0_0x0_0_0 | pad | bytes 2883588 | tf_op jit(solution)/shard_map/slice | solution.py:98
  243.8 6.5 %pad.50 = f32[4,8,128,128]{3,2,1,0:T(8,128)} pad(f32[4,4,128,128]{3,2,1,0:T(8,128)S(1)} %pad_maximum_fusion.1, f32[]{:T(128)} %constant.8.clone.1), padding=0_0_0x0_1_1x0_0_0x0_0_0 | pad | bytes 3145732 | tf_op jit(solution)/shard_map/pad | solution.py:94
  250.2 6.3 %pad.119 = f32[4,7,128,128]{3,2,1,0:T(8,128)} pad(f32[4,4,128,128]{3,2,1,0:T(8,128)S(1)} %copy-done.7, f32[]{:T(128)} %constant.8.clone.1), padding=0_0_0x0_0_1x0_0_0x0_0_0 | pad | bytes 2883588
  256.6 6.5 %pad.45 = f32[4,8,128,128]{3,2,1,0:T(8,128)} pad(f32[4,4,128,128]{3,2,1,0:T(8,128)S(1)} %copy-done.7, f32[]{:T(128)} %constant.8.clone.1), padding=0_0_0x1_0_1x0_0_0x0_0_0 | pad | bytes 3145732 | tf_op jit(solution)/shard_map/pad | solution.py:94
  263.7 1.7 reshape.122
  265.4 6.5 %pad.51 = f32[4,8,128,128]{3,2,1,0:T(8,128)} pad(f32[4,4,128,128]{3,2,1,0:T(8,128)S(1)} %copy-done.19, f32[]{:T(128)} %constant.8.clone.1), padding=0_0_0x1_0_1x0_0_0x0_0_0 | pad | bytes 3145732 | tf_op jit(solution)/shard_map/pad | solution.py:94
  271.9 1.1 pad_maximum_fusion
  273.0 10.2 %pad.44 = f32[4,8,128,128]{3,2,1,0:T(8,128)} pad(f32[4,4,128,128]{3,2,1,0:T(8,128)} %pad_maximum_fusion, f32[]{:T(128)} %constant.8.clone.1), padding=0_0_0x0_1_1x0_0_0x0_0_0 | pad | bytes 3145732 | tf_op jit(solution)/shard_map/pad | solution.py:94
  283.2 3.1 slice_add_fusion.1
  286.3 1.9 add_bitcast_fusion
  288.3 1.7 add_bitcast_fusion.1
  289.9 1.0 fusion.21
  291.0 0.8 copy-done.22
  291.8 1.9 convolution_subtract_fusion
  293.7 1.5 slice_add_fusion
  295.2 44.5 %while.11 = (s32[]{:T(128)}, f32[4,128,128]{2,1,0:T(8,128)S(1)}, f32[4,128,128]{2,1,0:T(8,128)S(1)}, f32[4,128,128]{2,1,0:T(8,128)S(1)}, s32[]{:T(128)}, /*index=5*/s32[]{:T(128)}) while((s32[]{:T(128)}, f32[4,128,128]{2,1,0:T(8,128)S(1)}, f32[4,128,128]{2,1,0:T(8,128)S(1)}, f32[4,128,128]{2,1,0:T(8,128)S(1)}, s32[]{:T(128)}, ...), condition=%wide.region_3.4_spmd.clone, body=%wide.region_2.3_spmd.clone.sunk | while | flops 100925440 | bytes 1835127 | solution.py:109
  295.6 2.4 collective-permute-start
  297.9 1.0 collective-permute-done
  299.3 5.5 %collective-permute-start = (bf16[4,128,128]{2,1,0:T(8,128)(2,1)S(1)}, bf16[4,128,128]{2,1,0:T(8,128)(2,1)S(1)}, u32[]{:S(2)}, u32[]{:S(2)}) collective-permute-start(bf16[4,128,128]{2,1,0:T(8,128)(2,1)S(1)} %fusion.96), channel_id=1, source_target_pairs={{0,4},{4,8},{8,12},{12,16},{16,20},{20,24},{24,28},{1,5},{5,9},{9,... | collective-permute-start | bytes 393224 | tf_op jit(solution)/shard_map/while/body/eval_jaxpr/ppermute | solution.py:16
  304.8 1.0 collective-permute-done
  306.2 5.3 %collective-permute-start = (bf16[4,128,128]{2,1,0:T(8,128)(2,1)S(1)}, bf16[4,128,128]{2,1,0:T(8,128)(2,1)S(1)}, u32[]{:S(2)}, u32[]{:S(2)}) collective-permute-start(bf16[4,128,128]{2,1,0:T(8,128)(2,1)S(1)} %fusion.96), channel_id=1, source_target_pairs={{0,4},{4,8},{8,12},{12,16},{16,20},{20,24},{24,28},{1,5},{5,9},{9,... | collective-permute-start | bytes 393224 | tf_op jit(solution)/shard_map/while/body/eval_jaxpr/ppermute | solution.py:16
  311.6 1.0 collective-permute-done
  313.0 5.3 %collective-permute-start = (bf16[4,128,128]{2,1,0:T(8,128)(2,1)S(1)}, bf16[4,128,128]{2,1,0:T(8,128)(2,1)S(1)}, u32[]{:S(2)}, u32[]{:S(2)}) collective-permute-start(bf16[4,128,128]{2,1,0:T(8,128)(2,1)S(1)} %fusion.96), channel_id=1, source_target_pairs={{0,4},{4,8},{8,12},{12,16},{16,20},{20,24},{24,28},{1,5},{5,9},{9,... | collective-permute-start | bytes 393224 | tf_op jit(solution)/shard_map/while/body/eval_jaxpr/ppermute | solution.py:16
  318.3 1.0 collective-permute-done
  319.7 5.3 %collective-permute-start = (bf16[4,128,128]{2,1,0:T(8,128)(2,1)S(1)}, bf16[4,128,128]{2,1,0:T(8,128)(2,1)S(1)}, u32[]{:S(2)}, u32[]{:S(2)}) collective-permute-start(bf16[4,128,128]{2,1,0:T(8,128)(2,1)S(1)} %fusion.96), channel_id=1, source_target_pairs={{0,4},{4,8},{8,12},{12,16},{16,20},{20,24},{24,28},{1,5},{5,9},{9,... | collective-permute-start | bytes 393224 | tf_op jit(solution)/shard_map/while/body/eval_jaxpr/ppermute | solution.py:16
  325.0 1.0 collective-permute-done
  326.4 5.3 %collective-permute-start = (bf16[4,128,128]{2,1,0:T(8,128)(2,1)S(1)}, bf16[4,128,128]{2,1,0:T(8,128)(2,1)S(1)}, u32[]{:S(2)}, u32[]{:S(2)}) collective-permute-start(bf16[4,128,128]{2,1,0:T(8,128)(2,1)S(1)} %fusion.96), channel_id=1, source_target_pairs={{0,4},{4,8},{8,12},{12,16},{16,20},{20,24},{24,28},{1,5},{5,9},{9,... | collective-permute-start | bytes 393224 | tf_op jit(solution)/shard_map/while/body/eval_jaxpr/ppermute | solution.py:16
  331.7 1.0 collective-permute-done
  333.1 5.3 %collective-permute-start = (bf16[4,128,128]{2,1,0:T(8,128)(2,1)S(1)}, bf16[4,128,128]{2,1,0:T(8,128)(2,1)S(1)}, u32[]{:S(2)}, u32[]{:S(2)}) collective-permute-start(bf16[4,128,128]{2,1,0:T(8,128)(2,1)S(1)} %fusion.96), channel_id=1, source_target_pairs={{0,4},{4,8},{8,12},{12,16},{16,20},{20,24},{24,28},{1,5},{5,9},{9,... | collective-permute-start | bytes 393224 | tf_op jit(solution)/shard_map/while/body/eval_jaxpr/ppermute | solution.py:16
  338.5 1.0 collective-permute-done
  339.8 3.6 fusion.9
  343.4 1.9 fusion.13
  345.3 1.1 multiply_reduce_fusion
  347.0 2.6 convolution_convert_fusion
  349.6 54.9 %reduce-scatter.2.cloned.1.call-done = bf16[64,4096]{1,0:T(8,128)(2,1)} async-done(((bf16[256,4096]{1,0:T(8,128)(2,1)}), bf16[64,4096]{1,0:T(8,128)(2,1)}) %reduce-scatter.2.cloned.1.call-update) | async-done | bytes 524304 | tf_op jit(solution)/shard_map/reduce_scatter | solution.py:119
  (124 shorter events, 13.0 us)
Async XLA Ops:
  6.5 398.0 %reduce-scatter.2.cloned.1.call-start = ((), (), s32[]{:S(2)}) async-start(), calls=%async_computation.1 | async-start | bytes 2621440 | tf_op jit(solution)/shard_map/reduce_scatter | solution.py:119
  11.3 3.2 copy-start.21
  12.4 2.6 copy-start.27
  21.2 0.8 copy-start.29
  21.2 0.8 copy-start.30
  183.1 1.2 copy-start.25
  186.3 5.5 %copy-start.1 = (f32[4,8,64,256]{3,2,1,0:T(8,128)}, f32[4,8,64,256]{3,2,1,0:T(8,128)S(1)}, u32[]{:S(2)}) copy-start(f32[4,8,64,256]{3,2,1,0:T(8,128)S(1)} %fusion.5) | copy-start | bytes 6291460
  186.3 5.5 %copy-start.31 = (f32[4,8]{1,0:T(4,128)S(1)}, f32[4,8]{1,0:T(4,128)}, u32[]{:S(2)}) copy-start(f32[4,8]{1,0:T(4,128)} %exp.34) | copy-start | bytes 388
  196.1 37.4 %copy-start = (f32[4,8,128,128]{3,2,1,0:T(8,128)}, f32[4,8,128,128]{3,2,1,0:T(8,128)S(1)}, u32[]{:S(2)}) copy-start(f32[4,8,128,128]{3,2,1,0:T(8,128)S(1)} %multiply_subtract_fusion) | copy-start | bytes 6291460
  197.2 1.8 copy-start.3
  198.1 1.7 copy-start.17
  212.3 3.3 copy-start.10
  212.3 3.3 copy-start.11
  215.6 2.0 copy-start.8
  216.7 2.1 copy-start.4
  217.6 1.9 copy-start.18
  233.5 2.7 copy-start.12
  233.5 2.7 copy-start.13
  236.2 1.1 slice-start.1
  243.8 6.5 %copy-start.7 = (f32[4,4,128,128]{3,2,1,0:T(8,128)S(1)}, f32[4,4,128,128]{3,2,1,0:T(8,128)}, u32[]{:S(2)}) copy-start(f32[4,4,128,128]{3,2,1,0:T(8,128)} %add.140) | copy-start | bytes 3145732
  256.6 6.5 %copy-start.34 = (s32[32]{0:T(128)S(1)}, s32[32]{0:T(128)}, u32[]{:S(2)}) copy-start(s32[32]{0:T(128)} %multiply_add_fusion) | copy-start | bytes 388
  256.6 8.9 %copy-start.19 = (f32[4,4,128,128]{3,2,1,0:T(8,128)S(1)}, f32[4,4,128,128]{3,2,1,0:T(8,128)}, u32[]{:S(2)}) copy-start(f32[4,4,128,128]{3,2,1,0:T(8,128)} %add.147) | copy-start | bytes 3145732
  263.0 8.9 %slice-start = ((f32[4,8,128,128]{3,2,1,0:T(8,128)}), f32[4,1,128,128]{3,2,1,0:T(8,128)S(1)}, s32[]{:S(2)}) async-start(f32[4,8,128,128]{3,2,1,0:T(8,128)} %copy-done), calls=%async_computation.2 | async-start | bytes 524288 | tf_op jit(solution)/shard_map/slice | solution.py:94
  263.0 8.9 %copy-start.20 = (f32[4,3,128,128]{3,2,1,0:T(8,128)S(1)}, f32[4,3,128,128]{3,2,1,0:T(8,128)}, u32[]{:S(2)}) copy-start(f32[4,3,128,128]{3,2,1,0:T(8,128)} %fusion.44) | copy-start | bytes 2359300
  273.0 10.2 %copy-start.9 = (f32[4,8,128,128]{3,2,1,0:T(8,128)S(1)}, f32[4,8,128,128]{3,2,1,0:T(8,128)}, u32[]{:S(2)}) copy-start(f32[4,8,128,128]{3,2,1,0:T(8,128)} %pad.51) | copy-start | bytes 6291460
  283.2 6.7 %copy-start.26 = (bf16[8,32,4,128]{3,2,1,0:T(4,128)(2,1)S(1)}, bf16[8,32,4,128]{3,2,1,0:T(4,128)(2,1)}, u32[]{:S(2)}) copy-start(bf16[8,32,4,128]{3,2,1,0:T(4,128)(2,1)} %reshape.122) | copy-start | bytes 786436
  283.2 6.7 %copy-start.28 = (f32[4,8,64]{2,1,0:T(8,128)S(1)}, f32[4,8,64]{2,1,0:T(8,128)}, u32[]{:S(2)}) copy-start(f32[4,8,64]{2,1,0:T(8,128)} %copy-done.27) | copy-start | bytes 24580
  283.2 6.7 %copy-start.32 = (pred[32,64]{1,0:T(8,128)(4,1)S(1)}, pred[32,64]{1,0:T(8,128)(4,1)}, u32[]{:S(2)}) copy-start(pred[32,64]{1,0:T(8,128)(4,1)} %iota_compare_fusion.5) | copy-start | bytes 6148
  283.2 10.5 %copy-start.15 = (f32[4,8,128,128]{3,2,1,0:T(8,128)S(1)}, f32[4,8,128,128]{3,2,1,0:T(8,128)}, u32[]{:S(2)}) copy-start(f32[4,8,128,128]{3,2,1,0:T(8,128)} %pad.44) | copy-start | bytes 6291460
  286.3 5.5 %copy-start.2 = (f32[4,8,64,256]{3,2,1,0:T(8,128)S(1)}, f32[4,8,64,256]{3,2,1,0:T(8,128)}, u32[]{:S(2)}) copy-start(f32[4,8,64,256]{3,2,1,0:T(8,128)} %copy-done.1) | copy-start | bytes 6291460
  289.9 3.8 copy-start.14
  291.0 0.8 copy-start.22
  293.7 1.5 copy-start.5
  293.7 1.5 copy-start.6
  295.6 3.3 collective-permute-start
  299.3 6.4 %collective-permute-start = (bf16[4,128,128]{2,1,0:T(8,128)(2,1)S(1)}, bf16[4,128,128]{2,1,0:T(8,128)(2,1)S(1)}, u32[]{:S(2)}, u32[]{:S(2)}) collective-permute-start(bf16[4,128,128]{2,1,0:T(8,128)(2,1)S(1)} %fusion.96), channel_id=1, source_target_pairs={{0,4},{4,8},{8,12},{12,16},{16,20},{20,24},{24,28},{1,5},{5,9},{9,... | collective-permute-start | bytes 393224 | tf_op jit(solution)/shard_map/while/body/eval_jaxpr/ppermute | solution.py:16
  306.2 6.3 %collective-permute-start = (bf16[4,128,128]{2,1,0:T(8,128)(2,1)S(1)}, bf16[4,128,128]{2,1,0:T(8,128)(2,1)S(1)}, u32[]{:S(2)}, u32[]{:S(2)}) collective-permute-start(bf16[4,128,128]{2,1,0:T(8,128)(2,1)S(1)} %fusion.96), channel_id=1, source_target_pairs={{0,4},{4,8},{8,12},{12,16},{16,20},{20,24},{24,28},{1,5},{5,9},{9,... | collective-permute-start | bytes 393224 | tf_op jit(solution)/shard_map/while/body/eval_jaxpr/ppermute | solution.py:16
  313.0 6.3 %collective-permute-start = (bf16[4,128,128]{2,1,0:T(8,128)(2,1)S(1)}, bf16[4,128,128]{2,1,0:T(8,128)(2,1)S(1)}, u32[]{:S(2)}, u32[]{:S(2)}) collective-permute-start(bf16[4,128,128]{2,1,0:T(8,128)(2,1)S(1)} %fusion.96), channel_id=1, source_target_pairs={{0,4},{4,8},{8,12},{12,16},{16,20},{20,24},{24,28},{1,5},{5,9},{9,... | collective-permute-start | bytes 393224 | tf_op jit(solution)/shard_map/while/body/eval_jaxpr/ppermute | solution.py:16
  319.7 6.3 %collective-permute-start = (bf16[4,128,128]{2,1,0:T(8,128)(2,1)S(1)}, bf16[4,128,128]{2,1,0:T(8,128)(2,1)S(1)}, u32[]{:S(2)}, u32[]{:S(2)}) collective-permute-start(bf16[4,128,128]{2,1,0:T(8,128)(2,1)S(1)} %fusion.96), channel_id=1, source_target_pairs={{0,4},{4,8},{8,12},{12,16},{16,20},{20,24},{24,28},{1,5},{5,9},{9,... | collective-permute-start | bytes 393224 | tf_op jit(solution)/shard_map/while/body/eval_jaxpr/ppermute | solution.py:16
  326.4 6.3 %collective-permute-start = (bf16[4,128,128]{2,1,0:T(8,128)(2,1)S(1)}, bf16[4,128,128]{2,1,0:T(8,128)(2,1)S(1)}, u32[]{:S(2)}, u32[]{:S(2)}) collective-permute-start(bf16[4,128,128]{2,1,0:T(8,128)(2,1)S(1)} %fusion.96), channel_id=1, source_target_pairs={{0,4},{4,8},{8,12},{12,16},{16,20},{20,24},{24,28},{1,5},{5,9},{9,... | collective-permute-start | bytes 393224 | tf_op jit(solution)/shard_map/while/body/eval_jaxpr/ppermute | solution.py:16
  333.1 6.3 %collective-permute-start = (bf16[4,128,128]{2,1,0:T(8,128)(2,1)S(1)}, bf16[4,128,128]{2,1,0:T(8,128)(2,1)S(1)}, u32[]{:S(2)}, u32[]{:S(2)}) collective-permute-start(bf16[4,128,128]{2,1,0:T(8,128)(2,1)S(1)} %fusion.96), channel_id=1, source_target_pairs={{0,4},{4,8},{8,12},{12,16},{16,20},{20,24},{24,28},{1,5},{5,9},{9,... | collective-permute-start | bytes 393224 | tf_op jit(solution)/shard_map/while/body/eval_jaxpr/ppermute | solution.py:16
  339.7 3.6 copy-start.16
  339.8 3.6 copy-start.24
  343.4 2.0 copy-start.23
  343.4 3.6 copy-start.35
  345.3 1.2 copy-start.33
Sparse Core Ops, SparseCore 0:
  349.7 54.7 reduce-scatter.1
where the time goes:
time: 420 us; the launch traced here: 412 us
  other arithmetic  181 us (43%)
  local copies, waits for them, and re-layouts  78.5 us (19%)
  waiting for transfers between devices  61.6 us (15%)
  matrix products  41.1 us (10%)
  starting transfers between devices  34.4 us (8%)
  between operations  14.4 us (3%)
    another operation x2, other arithmetic, span_terms(): lax.linalg.triangular_solve(system, right_side, left_side=True, lower=Tru...  158 us
    reduce_scatter x1, waiting for transfers between devices, on_device(): lax.psum_scatter(jnp.dot(flat_rows, out_weight, preferred_element_type=jn...  54.9 us
    pad x8, local copies, waits for them, and re-layouts, on_device(): inclusive = lax.associative_scan(combine_maps, (transition, offset), axis=1)  52.7 us
    ppermute x7, starting transfers between devices, shifted(): return lax.ppermute(block, axis, route)  34.4 us
    unnamed x74, local copies, waits for them, and re-layouts  9.74 us
    add x6, other arithmetic, on_device(): inclusive = lax.associative_scan(combine_maps, (transition, offset), axis=1)  8.5 us
  transfers between devices with their start and end apart: 8, of which 8 were waited for; matrix products, arithmetic and copies ran while one was open for 0% of the time, Pallas kernels for 0%

commit v1 on v0

v1 whole, which is shorter than its diff:
```python
import functools

import jax
import jax.numpy as jnp
from jax import lax
from jax.experimental import pallas as pl
from jax.experimental.pallas import tpu as pltpu
from jax.sharding import PartitionSpec as P

DH = 128
F32 = jnp.float32
BF16 = jnp.bfloat16
highest = lax.Precision.HIGHEST


def mm(a, b):
    return jnp.dot(a, b, preferred_element_type=F32)


def halves(x):
    high = x.astype(BF16)
    return high, (x - high.astype(F32)).astype(BF16)


def mm_split(a, b):
    a_high, a_low = halves(a)
    b_high, b_low = halves(b)
    left = jnp.concatenate([a_high, a_low], axis=1)
    row = jnp.concatenate([b_high, b_low], axis=1)
    wide = mm(left, jnp.concatenate([row, row], axis=0))
    n = b.shape[1]
    return wide[:, :n] + wide[:, n:]


def iota(shape, axis):
    return lax.broadcasted_iota(jnp.int32, shape, axis)


def local_kernel(heads, tokens, q_ref, k_ref, v_ref, beta_ref, gate_ref, lead_ref, loc_ref, m_ref, o_ref):
    span = 64 if tokens % 64 == 0 else tokens
    steps = 2 * span
    chunks = tokens // span
    gate = jnp.maximum(gate_ref[...], -1000.0)
    t_at, s_at = iota((tokens, 2 * tokens), 0), iota((tokens, 2 * tokens), 1)
    same = (t_at // span) == (s_at // steps)
    until = (same & (2 * t_at <= s_at)).astype(F32)
    exact = functools.partial(jnp.dot, precision=highest, preferred_element_type=F32)
    cum = exact(gate, until)
    beta = exact(beta_ref[:, 0, :], (2 * t_at == s_at).astype(F32)) + exact(
        beta_ref[:, 1, :], (2 * t_at + 1 == s_at).astype(F32)
    )
    r_at, c_at = iota((tokens, tokens), 0), iota((tokens, tokens), 1)
    read = exact(gate, (((r_at // span) == (c_at // span)) & (r_at <= c_at)).astype(F32))
    pad = jnp.zeros((8 - heads % 8, 2 * tokens), F32) if heads % 8 else None
    if pad is not None:
        cum_columns = jnp.concatenate([cum, pad], axis=0).T
        read_columns = jnp.concatenate([read, pad[:, :tokens]], axis=0).T
        beta_columns = jnp.concatenate([beta, pad], axis=0).T
    else:
        cum_columns, read_columns, beta_columns = cum.T, read.T, beta.T

    row, col = iota((steps, steps), 0), iota((steps, steps), 1)
    eye, strict = row == col, row > col
    levels = []
    size = 1
    while size < steps:
        levels.append(((row // size) % 2 == 1) & ((row // size) - 1 == col // size))
        size *= 2
    token = iota((span, steps), 0)
    visible = 2 * token + 1 >= iota((span, steps), 1)

    blocks = [(h, c) for c in range(chunks) for h in range(heads)]

    def cut(h, c):
        k = k_ref[c * steps : (c + 1) * steps, h * DH : (h + 1) * DH]
        q = q_ref[c * span : (c + 1) * span, h * DH : (h + 1) * DH]
        v = v_ref[c * steps : (c + 1) * steps, h * DH : (h + 1) * DH]
        return q, k, v

    data = {}
    for h, c in blocks:
        q, k, v = cut(h, c)
        inner = lax.dot_general(
            jnp.concatenate([k, q], axis=0), k, (((1,), (1,)), ((), ())), preferred_element_type=F32
        )
        key_inner, query_inner = inner[:steps], inner[steps:]
        diag = jnp.where(eye, key_inner, 0.0)
        scale_row = lax.rsqrt(jnp.sum(diag, axis=0, keepdims=True) + 1e-06)
        scale_col = lax.rsqrt(jnp.sum(diag, axis=1, keepdims=True) + 1e-06)
        cum_row = cum[h : h + 1, c * steps : (c + 1) * steps]
        cum_col = cum_columns[c * steps : (c + 1) * steps, h : h + 1]
        read_col = read_columns[c * span : (c + 1) * span, h : h + 1]
        beta_row = beta[h : h + 1, c * steps : (c + 1) * steps]
        beta_col = beta_columns[c * steps : (c + 1) * steps, h : h + 1]
        weight_row = beta_row * scale_row
        gaps = jnp.exp(jnp.where(strict, cum_col - cum_row, 0.0))
        lower = jnp.where(strict, gaps * key_inner * scale_col * weight_row, 0.0)
        gaps = jnp.exp(jnp.where(visible, read_col - cum_row, 0.0))
        scores = jnp.where(visible, gaps * query_inner * weight_row, 0.0)
        total = cum[h : h + 1, (c + 1) * steps - 1 : (c + 1) * steps]
        into = jnp.exp(total - cum_col) * beta_col * scale_col
        inverse = jnp.where(eye, 1.0, 0.0) - jnp.where(levels[0], lower, 0.0)
        data[h, c] = dict(
            lower=lower, inverse=inverse, scores=scores, into=into, total=jnp.exp(total),
            read=jnp.exp(read_col), carry=jnp.exp(cum_row) * scale_row,
        )
    for level in levels[1:]:
        for b in blocks:
            d = data[b]
            d["part"] = mm_split(jnp.where(level, d["lower"], 0.0), d["inverse"])
        for b in blocks:
            d = data[b]
            d["inverse"] = d["inverse"] - mm_split(d["inverse"], d["part"])
    for h, c in blocks:
        d = data[h, c]
        q, k, v = cut(h, c)
        high, low = halves(d["inverse"])
        d["fresh"] = mm(jnp.concatenate([high, low], axis=1), jnp.concatenate([v, v], axis=0))
        high, low = halves(d["inverse"] * d["carry"])
        d["carried"] = mm(jnp.concatenate([high, low], axis=1), jnp.concatenate([k, k], axis=0))

    zero = jnp.zeros((steps, DH), F32)
    state = [jnp.concatenate([jnp.where(iota((DH, DH), 0) == iota((DH, DH), 1), 1.0, 0.0), jnp.zeros((DH, DH), F32)], axis=1)] * heads
    for c in range(chunks):
        for h in range(heads):
            d = data[h, c]
            q, k, v = cut(h, c)
            s_high, s_low = halves(state[h])
            w_high, w_low = halves(d["carried"])
            moved = mm(
                jnp.concatenate([w_high, w_low], axis=1), jnp.concatenate([s_high, s_high], axis=0)
            ) + mm(w_high, s_low)
            new = jnp.concatenate([zero, d["fresh"]], axis=1) - moved
            seen = d["read"] * (mm(q, s_high) + mm(q, s_low)) + mm(d["scores"].astype(BF16), new.astype(BF16))
            rows = slice(c * span, (c + 1) * span)
            lead_ref[h, rows, :] = seen[:, :DH].astype(BF16)
            loc_ref[h, rows, :] = seen[:, DH:]
            n_high, n_low = halves(new * d["into"])
            turned = k.T
            state[h] = d["total"] * state[h] + mm(
                jnp.concatenate([turned, turned], axis=1), jnp.concatenate([n_high, n_low], axis=0)
            )
    for h in range(heads):
        m_ref[h] = state[h][:, :DH]
        o_ref[h] = state[h][:, DH:]


def local_terms(queries, keys, values, beta, log_gate):
    heads, tokens = log_gate.shape
    shape = jax.ShapeDtypeStruct
    return pl.pallas_call(
        functools.partial(local_kernel, heads, tokens),
        out_shape=(
            shape((heads, tokens, DH), BF16),
            shape((heads, tokens, DH), F32),
            shape((heads, DH, DH), F32),
            shape((heads, DH, DH), F32),
        ),
        in_specs=[pl.BlockSpec(memory_space=pltpu.VMEM)] * 5,
        out_specs=[pl.BlockSpec(memory_space=pltpu.VMEM)] * 4,
        compiler_params=pltpu.CompilerParams(vmem_limit_bytes=40 * 2**20),
        name="local_terms",
    )(queries, keys.reshape(2 * tokens, -1), values.reshape(2 * tokens, -1), beta, log_gate)


def shifted(block, axis, distance):
    devices = range(lax.axis_size(axis))
    route = [(i - distance, i) for i in devices if i - distance in devices]
    return lax.ppermute(block, axis, route)


def on_device(queries, keys, values, beta, log_gate, norm_gain, out_weight):
    heads, tokens = log_gate.shape
    lead, local_part, device_map, device_offset = local_terms(queries, keys, values, beta, log_gate)

    def relay_state(turn_index, incoming):
        leaving = (
            jnp.einsum("hij,hjk->hik", device_map, incoming, precision=highest) + device_offset
        )
        return shifted(leaving.astype(BF16), "ctx", 1).astype(leaving.dtype)

    incoming = lax.fori_loop(
        0, lax.axis_size("ctx") - 1, relay_state, jnp.zeros((heads, DH, DH), F32)
    )
    read_rows = jnp.einsum("htd,hde->hte", lead, incoming.astype(BF16), preferred_element_type=F32) + local_part
    row_scale = lax.rsqrt(jnp.mean(read_rows * read_rows, axis=-1, keepdims=True) + 1e-06)
    normed = (read_rows * row_scale * norm_gain.reshape(heads, 1, DH)).astype(BF16)
    flat_rows = jnp.transpose(normed, (1, 0, 2)).reshape(tokens, heads * DH)
    return lax.psum_scatter(
        jnp.dot(flat_rows, out_weight, preferred_element_type=F32).astype(BF16),
        "head",
        scatter_dimension=0,
        tiled=True,
    )


def solution(mesh):
    return jax.shard_map(
        on_device,
        mesh=mesh,
        in_specs=(
            P("ctx", "head"),
            P("ctx", None, "head"),
            P("ctx", None, "head"),
            P("head", None, "ctx"),
            P("head", "ctx"),
            P("head"),
            P("head", None),
        ),
        out_specs=P(("ctx", "head"), None),
        check_vma=False,
    )
```

time: 420 us -> 134 us (0.32)
  the two profiles are of different devices: /device:TPU:0 before, /device:TPU:6 now
where the time goes in v1:
time: 134 us; the launch traced here: 131 us
  waiting for transfers between devices  81.1 us (61%)
  between operations  13.5 us (10%)
  starting transfers between devices  13.4 us (10%)
  Pallas kernels  9.95 us (7%)
  matrix products  7.94 us (6%)
  local copies, waits for them, and re-layouts  4.96 us (4%)
    reduce_scatter x1, waiting for transfers between devices, on_device(): lax.psum_scatter(jnp.dot(flat_rows, out_weight, preferred_element_type=F3...  50.6 us
    ppermute x7, waiting for transfers between devices, shifted(): return lax.ppermute(block, axis, route)  30.5 us
    ppermute x7, starting transfers between devices, shifted(): return lax.ppermute(block, axis, route)  13.4 us
    pallas_call x1, Pallas kernels, local_terms(): pl.pallas_call(functools.partial(local_kernel, heads, tokens), out_shape=...  9.95 us
    dot_general x1, matrix products, on_device(): jnp.dot(flat_rows, out_weight, preferred_element_type=F32).astype(BF16)  4.81 us
    dot_general x7, matrix products, relay_state(): jnp.einsum('hij,hjk->hik', device_map, incoming, precision=highest)  2.75 us
  transfers between devices with their start and end apart: 8, of which 8 were waited for; matrix products, arithmetic and copies ran while one was open for 0% of the time, Pallas kernels for 0%

profile of v1, /device:TPU:6, one launch (start us, length us, event | category | flops | bytes accessed | tf_op | source)
XLA Modules:
  0.0 131.4 jit_solution(2672433688561812137)
XLA Ops:
  6.5 0.0 reduce-scatter.2.cloned.1.call-start
  6.5 1.2 reshape.19.k_ref
  7.8 1.2 reshape.20.v_ref
  9.0 0.0 copy-start
  9.0 0.9 copy-done
  10.0 0.0 copy-start.1
  10.0 0.7 copy-done.1
  10.7 0.0 copy-start.2
  10.7 0.7 copy-done.2
  11.4 9.9 %local_terms.1 = (bf16[4,256,128]{2,1,0:T(8,128)(2,1)S(1)}, f32[4,256,128]{2,1,0:T(8,128)S(1)}, f32[4,128,128]{2,1,0:T(8,128)S(1)}, f32[4,128,128]{2,1,0:T(8,128)S(1)}) custom-call(bf16[256,512]{1,0:T(8,128)(2,1)S(1)} %copy-done, bf16[512,512]{1,0:T(8,128)(2,1)S(1)} %reshape.19.k_ref, bf16[512,512]{1,0:T(8,128)(2,1)S(1)} %reshape.20.v_ref, ...), custom_call_target="tpu_custom_call" | custom-call | tf_op jit(solution)/shard_map/local_terms/pallas_call | solution.py:151
  21.3 0.0 copy-start.3
  21.3 47.1 %while.11 = (s32[]{:T(128)}, f32[4,128,128]{2,1,0:T(8,128)S(1)}, f32[4,128,128]{2,1,0:T(8,128)S(1)}, f32[4,128,128]{2,1,0:T(8,128)S(1)}, s32[]{:T(128)}, /*index=5*/s32[]{:T(128)}) while((s32[]{:T(128)}, f32[4,128,128]{2,1,0:T(8,128)S(1)}, f32[4,128,128]{2,1,0:T(8,128)S(1)}, f32[4,128,128]{2,1,0:T(8,128)S(1)}, s32[]{:T(128)}, ...), condition=%wide.region_1.0_spmd.clone, body=%wide.region_0.0_spmd.clone.sunk | while | flops 100925440 | bytes 1835127 | solution.py:182
  21.3 0.4 fusion.16
  21.7 1.9 %collective-permute-start = (bf16[4,128,128]{2,1,0:T(8,128)(2,1)S(1)}, bf16[4,128,128]{2,1,0:T(8,128)(2,1)S(1)}, u32[]{:S(2)}, u32[]{:S(2)}) collective-permute-start(bf16[4,128,128]{2,1,0:T(8,128)(2,1)S(1)} %fusion.16), channel_id=1, source_target_pairs={{0,4},{4,8},{8,12},{12,16},{16,20},{20,24},{24,28},{1,5},{5,9},{9,... | collective-permute-start | bytes 393224 | tf_op jit(solution)/shard_map/while/body/eval_jaxpr/ppermute | solution.py:169
  23.7 4.4 %collective-permute-done = bf16[4,128,128]{2,1,0:T(8,128)(2,1)S(1)} collective-permute-done((bf16[4,128,128]{2,1,0:T(8,128)(2,1)S(1)}, bf16[4,128,128]{2,1,0:T(8,128)(2,1)S(1)}, u32[]{:S(2)}, u32[]{:S(2)}) %collective-permute-start) | collective-permute-done | bytes 131104 | tf_op jit(solution)/shard_map/while/body/eval_jaxpr/ppermute | solution.py:169
  28.1 0.4 fusion.16
  28.5 1.9 %collective-permute-start = (bf16[4,128,128]{2,1,0:T(8,128)(2,1)S(1)}, bf16[4,128,128]{2,1,0:T(8,128)(2,1)S(1)}, u32[]{:S(2)}, u32[]{:S(2)}) collective-permute-start(bf16[4,128,128]{2,1,0:T(8,128)(2,1)S(1)} %fusion.16), channel_id=1, source_target_pairs={{0,4},{4,8},{8,12},{12,16},{16,20},{20,24},{24,28},{1,5},{5,9},{9,... | collective-permute-start | bytes 393224 | tf_op jit(solution)/shard_map/while/body/eval_jaxpr/ppermute | solution.py:169
  30.4 4.4 %collective-permute-done = bf16[4,128,128]{2,1,0:T(8,128)(2,1)S(1)} collective-permute-done((bf16[4,128,128]{2,1,0:T(8,128)(2,1)S(1)}, bf16[4,128,128]{2,1,0:T(8,128)(2,1)S(1)}, u32[]{:S(2)}, u32[]{:S(2)}) %collective-permute-start) | collective-permute-done | bytes 131104 | tf_op jit(solution)/shard_map/while/body/eval_jaxpr/ppermute | solution.py:169
  34.8 0.4 fusion.16
  35.2 1.9 %collective-permute-start = (bf16[4,128,128]{2,1,0:T(8,128)(2,1)S(1)}, bf16[4,128,128]{2,1,0:T(8,128)(2,1)S(1)}, u32[]{:S(2)}, u32[]{:S(2)}) collective-permute-start(bf16[4,128,128]{2,1,0:T(8,128)(2,1)S(1)} %fusion.16), channel_id=1, source_target_pairs={{0,4},{4,8},{8,12},{12,16},{16,20},{20,24},{24,28},{1,5},{5,9},{9,... | collective-permute-start | bytes 393224 | tf_op jit(solution)/shard_map/while/body/eval_jaxpr/ppermute | solution.py:169
  37.1 4.4 %collective-permute-done = bf16[4,128,128]{2,1,0:T(8,128)(2,1)S(1)} collective-permute-done((bf16[4,128,128]{2,1,0:T(8,128)(2,1)S(1)}, bf16[4,128,128]{2,1,0:T(8,128)(2,1)S(1)}, u32[]{:S(2)}, u32[]{:S(2)}) %collective-permute-start) | collective-permute-done | bytes 131104 | tf_op jit(solution)/shard_map/while/body/eval_jaxpr/ppermute | solution.py:169
  41.5 0.4 fusion.16
  41.9 1.9 %collective-permute-start = (bf16[4,128,128]{2,1,0:T(8,128)(2,1)S(1)}, bf16[4,128,128]{2,1,0:T(8,128)(2,1)S(1)}, u32[]{:S(2)}, u32[]{:S(2)}) collective-permute-start(bf16[4,128,128]{2,1,0:T(8,128)(2,1)S(1)} %fusion.16), channel_id=1, source_target_pairs={{0,4},{4,8},{8,12},{12,16},{16,20},{20,24},{24,28},{1,5},{5,9},{9,... | collective-permute-start | bytes 393224 | tf_op jit(solution)/shard_map/while/body/eval_jaxpr/ppermute | solution.py:169
  43.9 4.4 %collective-permute-done = bf16[4,128,128]{2,1,0:T(8,128)(2,1)S(1)} collective-permute-done((bf16[4,128,128]{2,1,0:T(8,128)(2,1)S(1)}, bf16[4,128,128]{2,1,0:T(8,128)(2,1)S(1)}, u32[]{:S(2)}, u32[]{:S(2)}) %collective-permute-start) | collective-permute-done | bytes 131104 | tf_op jit(solution)/shard_map/while/body/eval_jaxpr/ppermute | solution.py:169
  48.3 0.4 fusion.16
  48.7 1.9 %collective-permute-start = (bf16[4,128,128]{2,1,0:T(8,128)(2,1)S(1)}, bf16[4,128,128]{2,1,0:T(8,128)(2,1)S(1)}, u32[]{:S(2)}, u32[]{:S(2)}) collective-permute-start(bf16[4,128,128]{2,1,0:T(8,128)(2,1)S(1)} %fusion.16), channel_id=1, source_target_pairs={{0,4},{4,8},{8,12},{12,16},{16,20},{20,24},{24,28},{1,5},{5,9},{9,... | collective-permute-start | bytes 393224 | tf_op jit(solution)/shard_map/while/body/eval_jaxpr/ppermute | solution.py:169
  50.6 4.4 %collective-permute-done = bf16[4,128,128]{2,1,0:T(8,128)(2,1)S(1)} collective-permute-done((bf16[4,128,128]{2,1,0:T(8,128)(2,1)S(1)}, bf16[4,128,128]{2,1,0:T(8,128)(2,1)S(1)}, u32[]{:S(2)}, u32[]{:S(2)}) %collective-permute-start) | collective-permute-done | bytes 131104 | tf_op jit(solution)/shard_map/while/body/eval_jaxpr/ppermute | solution.py:169
  55.0 0.4 fusion.16
  55.4 1.9 %collective-permute-start = (bf16[4,128,128]{2,1,0:T(8,128)(2,1)S(1)}, bf16[4,128,128]{2,1,0:T(8,128)(2,1)S(1)}, u32[]{:S(2)}, u32[]{:S(2)}) collective-permute-start(bf16[4,128,128]{2,1,0:T(8,128)(2,1)S(1)} %fusion.16), channel_id=1, source_target_pairs={{0,4},{4,8},{8,12},{12,16},{16,20},{20,24},{24,28},{1,5},{5,9},{9,... | collective-permute-start | bytes 393224 | tf_op jit(solution)/shard_map/while/body/eval_jaxpr/ppermute | solution.py:169
  57.3 4.4 %collective-permute-done = bf16[4,128,128]{2,1,0:T(8,128)(2,1)S(1)} collective-permute-done((bf16[4,128,128]{2,1,0:T(8,128)(2,1)S(1)}, bf16[4,128,128]{2,1,0:T(8,128)(2,1)S(1)}, u32[]{:S(2)}, u32[]{:S(2)}) %collective-permute-start) | collective-permute-done | bytes 131104 | tf_op jit(solution)/shard_map/while/body/eval_jaxpr/ppermute | solution.py:169
  61.7 0.4 fusion.16
  62.1 1.9 %collective-permute-start = (bf16[4,128,128]{2,1,0:T(8,128)(2,1)S(1)}, bf16[4,128,128]{2,1,0:T(8,128)(2,1)S(1)}, u32[]{:S(2)}, u32[]{:S(2)}) collective-permute-start(bf16[4,128,128]{2,1,0:T(8,128)(2,1)S(1)} %fusion.16), channel_id=1, source_target_pairs={{0,4},{4,8},{8,12},{12,16},{16,20},{20,24},{24,28},{1,5},{5,9},{9,... | collective-permute-start | bytes 393224 | tf_op jit(solution)/shard_map/while/body/eval_jaxpr/ppermute | solution.py:169
  64.0 4.4 %collective-permute-done = bf16[4,128,128]{2,1,0:T(8,128)(2,1)S(1)} collective-permute-done((bf16[4,128,128]{2,1,0:T(8,128)(2,1)S(1)}, bf16[4,128,128]{2,1,0:T(8,128)(2,1)S(1)}, u32[]{:S(2)}, u32[]{:S(2)}) %collective-permute-start) | collective-permute-done | bytes 131104 | tf_op jit(solution)/shard_map/while/body/eval_jaxpr/ppermute | solution.py:169
  68.4 0.4 multiply_reduce_fusion
  68.8 0.0 copy-done.3
  68.8 0.2 fusion.5
  69.0 0.1 copy.12
  69.2 4.8 %convolution_convert_fusion = bf16[256,4096]{1,0:T(8,128)(2,1)} fusion(bf16[256,512]{0,1:T(8,128)(2,1)S(1)} %bitcast.10, bf16[512,4096]{1,0:T(8,128)(2,1)} %param.15), kind=kOutput, calls=%fused_computation.6 | convolution fusion | flops 1074790400 | bytes 6553600 | tf_op jit(solution)/shard_map/dot_general | solution.py:190
  74.0 0.0 reduce-scatter.2.cloned.1.call-update
  74.0 50.6 %reduce-scatter.2.cloned.1.call-done = bf16[64,4096]{1,0:T(8,128)(2,1)} async-done(((bf16[256,4096]{1,0:T(8,128)(2,1)}), bf16[64,4096]{1,0:T(8,128)(2,1)}) %reduce-scatter.2.cloned.1.call-update) | async-done | bytes 524304 | tf_op jit(solution)/shard_map/reduce_scatter | solution.py:189
  (9 shorter events, 0.1 us)
Async XLA Ops:
  6.5 118.1 %reduce-scatter.2.cloned.1.call-start = ((), (), s32[]{:S(2)}) async-start(), calls=%async_computation.1 | async-start | bytes 2621440 | tf_op jit(solution)/shard_map/reduce_scatter | solution.py:189
  9.0 1.0 copy-start
  10.0 0.7 copy-start.1
  10.7 0.7 copy-start.2
  21.3 47.5 %copy-start.3 = (f32[512]{0:T(512)S(1)}, f32[512]{0:T(512)}, u32[]{:S(2)}) copy-start(f32[512]{0:T(512)} %param.14) | copy-start | bytes 6148
  21.7 6.3 %collective-permute-start = (bf16[4,128,128]{2,1,0:T(8,128)(2,1)S(1)}, bf16[4,128,128]{2,1,0:T(8,128)(2,1)S(1)}, u32[]{:S(2)}, u32[]{:S(2)}) collective-permute-start(bf16[4,128,128]{2,1,0:T(8,128)(2,1)S(1)} %fusion.16), channel_id=1, source_target_pairs={{0,4},{4,8},{8,12},{12,16},{16,20},{20,24},{24,28},{1,5},{5,9},{9,... | collective-permute-start | bytes 393224 | tf_op jit(solution)/shard_map/while/body/eval_jaxpr/ppermute | solution.py:169
  28.5 6.3 %collective-permute-start = (bf16[4,128,128]{2,1,0:T(8,128)(2,1)S(1)}, bf16[4,128,128]{2,1,0:T(8,128)(2,1)S(1)}, u32[]{:S(2)}, u32[]{:S(2)}) collective-permute-start(bf16[4,128,128]{2,1,0:T(8,128)(2,1)S(1)} %fusion.16), channel_id=1, source_target_pairs={{0,4},{4,8},{8,12},{12,16},{16,20},{20,24},{24,28},{1,5},{5,9},{9,... | collective-permute-start | bytes 393224 | tf_op jit(solution)/shard_map/while/body/eval_jaxpr/ppermute | solution.py:169
  35.2 6.3 %collective-permute-start = (bf16[4,128,128]{2,1,0:T(8,128)(2,1)S(1)}, bf16[4,128,128]{2,1,0:T(8,128)(2,1)S(1)}, u32[]{:S(2)}, u32[]{:S(2)}) collective-permute-start(bf16[4,128,128]{2,1,0:T(8,128)(2,1)S(1)} %fusion.16), channel_id=1, source_target_pairs={{0,4},{4,8},{8,12},{12,16},{16,20},{20,24},{24,28},{1,5},{5,9},{9,... | collective-permute-start | bytes 393224 | tf_op jit(solution)/shard_map/while/body/eval_jaxpr/ppermute | solution.py:169
  41.9 6.3 %collective-permute-start = (bf16[4,128,128]{2,1,0:T(8,128)(2,1)S(1)}, bf16[4,128,128]{2,1,0:T(8,128)(2,1)S(1)}, u32[]{:S(2)}, u32[]{:S(2)}) collective-permute-start(bf16[4,128,128]{2,1,0:T(8,128)(2,1)S(1)} %fusion.16), channel_id=1, source_target_pairs={{0,4},{4,8},{8,12},{12,16},{16,20},{20,24},{24,28},{1,5},{5,9},{9,... | collective-permute-start | bytes 393224 | tf_op jit(solution)/shard_map/while/body/eval_jaxpr/ppermute | solution.py:169
  48.7 6.3 %collective-permute-start = (bf16[4,128,128]{2,1,0:T(8,128)(2,1)S(1)}, bf16[4,128,128]{2,1,0:T(8,128)(2,1)S(1)}, u32[]{:S(2)}, u32[]{:S(2)}) collective-permute-start(bf16[4,128,128]{2,1,0:T(8,128)(2,1)S(1)} %fusion.16), channel_id=1, source_target_pairs={{0,4},{4,8},{8,12},{12,16},{16,20},{20,24},{24,28},{1,5},{5,9},{9,... | collective-permute-start | bytes 393224 | tf_op jit(solution)/shard_map/while/body/eval_jaxpr/ppermute | solution.py:169
  55.4 6.3 %collective-permute-start = (bf16[4,128,128]{2,1,0:T(8,128)(2,1)S(1)}, bf16[4,128,128]{2,1,0:T(8,128)(2,1)S(1)}, u32[]{:S(2)}, u32[]{:S(2)}) collective-permute-start(bf16[4,128,128]{2,1,0:T(8,128)(2,1)S(1)} %fusion.16), channel_id=1, source_target_pairs={{0,4},{4,8},{8,12},{12,16},{16,20},{20,24},{24,28},{1,5},{5,9},{9,... | collective-permute-start | bytes 393224 | tf_op jit(solution)/shard_map/while/body/eval_jaxpr/ppermute | solution.py:169
  62.1 6.3 %collective-permute-start = (bf16[4,128,128]{2,1,0:T(8,128)(2,1)S(1)}, bf16[4,128,128]{2,1,0:T(8,128)(2,1)S(1)}, u32[]{:S(2)}, u32[]{:S(2)}) collective-permute-start(bf16[4,128,128]{2,1,0:T(8,128)(2,1)S(1)} %fusion.16), channel_id=1, source_target_pairs={{0,4},{4,8},{8,12},{12,16},{16,20},{20,24},{24,28},{1,5},{5,9},{9,... | collective-permute-start | bytes 393224 | tf_op jit(solution)/shard_map/while/body/eval_jaxpr/ppermute | solution.py:169
Sparse Core Ops, SparseCore 0:
  74.2 50.3 reduce-scatter.1

commit v2 on v1

--- a/solution.py
+++ b/solution.py
@@ -163,40 +163,230 @@
     )(queries, keys.reshape(2 * tokens, -1), values.reshape(2 * tokens, -1), beta, log_gate)
 
 
-def shifted(block, axis, distance):
-    devices = range(lax.axis_size(axis))
-    route = [(i - distance, i) for i in devices if i - distance in devices]
-    return lax.ppermute(block, axis, route)
-
-
-def on_device(queries, keys, values, beta, log_gate, norm_gain, out_weight):
-    heads, tokens = log_gate.shape
-    lead, local_part, device_map, device_offset = local_terms(queries, keys, values, beta, log_gate)
-
-    def relay_state(turn_index, incoming):
-        leaving = (
-            jnp.einsum("hij,hjk->hik", device_map, incoming, precision=highest) + device_offset
+def finish_kernel(
+    n_ctx, n_head, lead_ref, loc_ref, m_ref, o_ref, gain_ref, w_hbm, out_ref,
+    pair_send, pair_recv, joined, state_recv, state_send, normed, weight, part, recv,
+    weight_sem, pair_send_sem, pair_recv_sem, state_send_sem, state_recv_sem, row_send_sem, row_recv_sem,
+):
+    heads = lead_ref.shape[0]
+    pieces, _, block, width = part.shape
+    me = lax.axis_index("ctx")
+    at = lax.axis_index("head")
+    odd = lax.rem(me, 2) == 1
+    has_prev, has_next = me >= 2, me < n_ctx - 2
+
+    barrier = pltpu.get_barrier_semaphore()
+    around = [
+        (me >= 1, {"ctx": me - 1}),
+        (me < n_ctx - 1, {"ctx": me + 1}),
+        (odd & has_prev, {"ctx": me - 2}),
+        (odd & has_next, {"ctx": me + 2}),
+        (at >= 1, {"head": at - 1}),
+        (at < n_head - 1, {"head": at + 1}),
+    ]
+    count = 0
+    for there, device in around:
+        count = count + jnp.where(there, 1, 0)
+
+        @pl.when(there)
+        def _(device=device):
+            pl.semaphore_signal(barrier, inc=1, device_id=device, device_id_type=pl.DeviceIdType.MESH)
+
+    load = pltpu.make_async_copy(w_hbm, weight, weight_sem)
+    load.start()
+    pl.semaphore_wait(barrier, count)
+
+    def remote(src, dst, send_sem, recv_sem, device):
+        return pltpu.make_async_remote_copy(
+            src_ref=src, dst_ref=dst, send_sem=send_sem, recv_sem=recv_sem,
+            device_id=device, device_id_type=pl.DeviceIdType.MESH,
         )
-        return shifted(leaving.astype(BF16), "ctx", 1).astype(leaving.dtype)
-
-    incoming = lax.fori_loop(
-        0, lax.axis_size("ctx") - 1, relay_state, jnp.zeros((heads, DH, DH), F32)
-    )
-    read_rows = jnp.einsum("htd,hde->hte", lead, incoming.astype(BF16), preferred_element_type=F32) + local_part
-    row_scale = lax.rsqrt(jnp.mean(read_rows * read_rows, axis=-1, keepdims=True) + 1e-06)
-    normed = (read_rows * row_scale * norm_gain.reshape(heads, 1, DH)).astype(BF16)
-    flat_rows = jnp.transpose(normed, (1, 0, 2)).reshape(tokens, heads * DH)
-    return lax.psum_scatter(
-        jnp.dot(flat_rows, out_weight, preferred_element_type=F32).astype(BF16),
-        "head",
-        scatter_dimension=0,
-        tiled=True,
-    )
+
+    def pair_copy(h):
+        return remote(pair_send.at[h], pair_recv.at[h], pair_send_sem.at[h], pair_recv_sem.at[h], {"ctx": me + 1})
+
+    def state_copy(h, ahead):
+        return remote(
+            state_send.at[h], state_recv.at[h], state_send_sem.at[ahead - 1, h], state_recv_sem.at[h], {"ctx": me + ahead}
+        )
+
+    @pl.when(jnp.logical_not(odd))
+    def _():
+        for h in range(heads):
+            pair_send[h, :, :DH] = m_ref[h].astype(BF16)
+            pair_send[h, :, DH:] = o_ref[h].astype(BF16)
+            pair_copy(h).start()
+
+    @pl.when(jnp.logical_not(has_prev))
+    def _():
+        state_recv[...] = jnp.zeros_like(state_recv)
+
+    @pl.when(odd)
+    def _():
+        for h in range(heads):
+            pair_copy(h).wait_recv()
+            high, low = halves(m_ref[h])
+            first = pair_recv[h]
+            joined[h] = mm(jnp.concatenate([high, low], axis=1), jnp.concatenate([first, first], axis=0))
+
+    @pl.when(odd & has_next)
+    def _():
+        for h in range(heads):
+            high, low = halves(joined[h, :, :DH])
+            both = jnp.concatenate([high, low], axis=1)
+            offset = joined[h, :, DH:] + o_ref[h]
+
+            @pl.when(has_prev)
+            def _():
+                state_copy(h, 2).wait_recv()
+
+            state = state_recv[h]
+            state_send[h] = (mm(both, jnp.concatenate([state, state], axis=0)) + offset).astype(BF16)
+            state_copy(h, 2).start()
+            state_copy(h, 1).start()
+
+    @pl.when(has_prev & jnp.logical_not(odd & has_next))
+    def _():
+        for h in range(heads):
+            state_copy(h, 2).wait_recv()
+
+    @pl.when(odd)
+    def _():
+        for h in range(heads):
+            state_recv[h] = (mm(pair_recv[h, :, :DH], state_recv[h]) + pair_recv[h, :, DH:].astype(F32)).astype(BF16)
+
+    for h in range(heads):
+        read = mm(lead_ref[h], state_recv[h]) + loc_ref[h]
+        scale = lax.rsqrt(jnp.mean(read * read, axis=-1, keepdims=True) + 1e-06)
+        columns = slice(h * DH, (h + 1) * DH)
+        normed[:, columns] = (read * scale * gain_ref[:, columns]).astype(BF16)
+    load.wait()
+
+    def row_copy(p, r, to, slot):
+        return remote(part.at[p, r], recv.at[p, slot], row_send_sem.at[p, r], row_recv_sem.at[p, slot], {"head": to})
+
+    def each_row(p, way):
+        for r in range(n_head):
+            @pl.when(at < r)
+            def _(r=r):
+                way(row_copy(p, r, at + 1, r))
+
+            @pl.when(at > r)
+            def _(r=r):
+                way(row_copy(p, r, at - 1, jnp.where(at - 1 == r, n_head, r)))
+
+    def add(p, r, slot):
+        row_copy(p, r, at, slot).wait_recv()
+        part[p, r] = (part[p, r].astype(F32) + recv[p, slot].astype(F32)).astype(BF16)
+
+    def piece(p, carry):
+        @pl.when(p >= 2)
+        def _():
+            each_row(p - 2, lambda copy: copy.wait_send())
+
+        columns = pl.ds(pl.multiple_of(p * width, width), width)
+        rows = mm(normed[...], weight[:, columns]).astype(BF16)
+        for r in range(n_head):
+            part[p, r] = rows[r * block : (r + 1) * block]
+        for j in range(1, n_head):
+            right, left = n_head - j, j - 1
+
+            @pl.when(at < right)
+            def _():
+                @pl.when(at >= 1)
+                def _():
+                    add(p, right, right)
+
+                row_copy(p, right, at + 1, right).start()
+
+            @pl.when(at > left)
+            def _():
+                @pl.when(at < n_head - 1)
+                def _():
+                    add(p, left, left)
+
+                row_copy(p, left, at - 1, jnp.where(at - 1 == left, n_head, left)).start()
+
+        return carry
+
+    lax.fori_loop(0, pieces, piece, 0)
+
+    def last(p, carry):
+        columns = pl.ds(pl.multiple_of(p * width, width), width)
+        for r in range(n_head):
+            @pl.when(at == r)
+            def _(r=r):
+                total = part[p, r].astype(F32)
+                if r >= 1:
+                    row_copy(p, r, at, r).wait_recv()
+                    total = total + recv[p, r].astype(F32)
+                if r < n_head - 1:
+                    row_copy(p, r, at, n_head).wait_recv()
+                    total = total + recv[p, n_head].astype(F32)
+                out_ref[:, columns] = total.astype(BF16)
+
+        return carry
+
+    lax.fori_loop(0, pieces, last, 0)
+    for p in range(max(pieces - 2, 0), pieces):
+        each_row(p, lambda copy: copy.wait_send())
+
+    @pl.when(jnp.logical_not(odd))
+    def _():
+        for h in range(heads):
+            pair_copy(h).wait_send()
+
+    @pl.when(odd & has_next)
+    def _():
+        for h in range(heads):
+            state_copy(h, 2).wait_send()
+            state_copy(h, 1).wait_send()
+
+
+def finish(n_ctx, n_head, lead, local_part, device_map, device_offset, norm_gain, out_weight):
+    heads, tokens, _ = lead.shape
+    columns = out_weight.shape[1]
+    pieces = 8 if columns % 1024 == 0 else 1
+    width, block = columns // pieces, tokens // n_head
+    dma = pltpu.SemaphoreType.DMA
+    return pl.pallas_call(
+        functools.partial(finish_kernel, n_ctx, n_head),
+        out_shape=jax.ShapeDtypeStruct((block, columns), BF16),
+        in_specs=[pl.BlockSpec(memory_space=pltpu.VMEM)] * 5 + [pl.BlockSpec(memory_space=pl.ANY)],
+        out_specs=pl.BlockSpec(memory_space=pltpu.VMEM),
+        scratch_shapes=[
+            pltpu.VMEM((heads, DH, 2 * DH), BF16),
+            pltpu.VMEM((heads, DH, 2 * DH), BF16),
+            pltpu.VMEM((heads, DH, 2 * DH), F32),
+            pltpu.VMEM((heads, DH, DH), BF16),
+            pltpu.VMEM((heads, DH, DH), BF16),
+            pltpu.VMEM((tokens, heads * DH), BF16),
+            pltpu.VMEM(out_weight.shape, BF16),
+            pltpu.VMEM((pieces, n_head, block, width), BF16),
+            pltpu.VMEM((pieces, n_head + 1, block, width), BF16),
+            dma(()),
+            dma((heads,)),
+            dma((heads,)),
+            dma((2, heads)),
+            dma((heads,)),
+            dma((pieces, n_head)),
+            dma((pieces, n_head + 1)),
+        ],
+        compiler_params=pltpu.CompilerParams(
+            collective_id=0, has_side_effects=True, vmem_limit_bytes=40 * 2**20
+        ),
+        name="finish",
+    )(lead, local_part, device_map, device_offset, norm_gain.reshape(1, -1), out_weight)
+
+
+def on_device(n_ctx, n_head, queries, keys, values, beta, log_gate, norm_gain, out_weight):
+    terms = local_terms(queries, keys, values, beta, log_gate)
+    return finish(n_ctx, n_head, *terms, norm_gain, out_weight)
 
 
 def solution(mesh):
     return jax.shard_map(
-        on_device,
+        functools.partial(on_device, mesh.shape["ctx"], mesh.shape["head"]),
         mesh=mesh,
         in_specs=(
             P("ctx", "head"),

time: 134 us -> 101 us (0.75); the launches traced: 131 us -> 100 us
  Pallas kernels: 9.95 us -> 91.9 us
  waiting for transfers between devices: 81.1 us -> 0 us
  between operations: 13.5 us -> 0.04 us
  starting transfers between devices: 13.4 us -> 0 us
  matrix products: 7.94 us -> 0 us
  local copies, waits for them, and re-layouts: 4.96 us -> 8.47 us
    pallas_call x0 -> x1, Pallas kernels: none -> 81.9 us  [finish(): pl.pallas_call(functools.partial(finish_kernel, n_ctx, n_head), out_shape...]
    reduce_scatter x1 -> x0, waiting for transfers between devices: 50.6 us -> none  [on_device(): lax.psum_scatter(jnp.dot(flat_rows, out_weight, preferred_element_type=F3...]
    ppermute x7 -> x0, waiting for transfers between devices: 30.5 us -> none  [shifted(): return lax.ppermute(block, axis, route)]
    ppermute x7 -> x0, starting transfers between devices: 13.4 us -> none  [shifted(): return lax.ppermute(block, axis, route)]
    dot_general x9 -> x0, matrix products: 7.94 us -> none  [the longest x1 4.81 us: on_device(): jnp.dot(flat_rows, out_weight, preferred_element_type=F32).astype(BF16)]
    unnamed x8 -> x11, local copies, waits for them, and re-layouts: 2.33 us -> 5.99 us
  transfers between devices with their start and end apart: 8 -> 0, of which waited for: 8 -> 0; matrix products, arithmetic and copies ran while one was open for 0% -> 0% of each run, Pallas kernels for 0% -> 0%
where the time goes in v2:
time: 101 us; the launch traced here: 100 us
  Pallas kernels  91.9 us (91%)
  local copies, waits for them, and re-layouts  8.47 us (8%)
    pallas_call x1, Pallas kernels, finish(): pl.pallas_call(functools.partial(finish_kernel, n_ctx, n_head), out_shape...  81.9 us
    pallas_call x1, Pallas kernels, local_terms(): pl.pallas_call(functools.partial(local_kernel, heads, tokens), out_shape=...  9.94 us
    unnamed x11, local copies, waits for them, and re-layouts  5.99 us

profile of v2, /device:TPU:6, one launch (start us, length us, event | category | flops | bytes accessed | tf_op | source)
XLA Modules:
  0.0 100.4 jit_solution(13642017027826388587)
XLA Ops:
  0.0 1.2 %reshape.9.k_ref = bf16[512,512]{1,0:T(8,128)(2,1)S(1)} reshape(bf16[256,2,512]{2,1,0:T(2,128)(2,1)} %param.8) | data formatting | bytes 1048576 | tf_op jit(solution)/shard_map/reshape | solution.py:163
  1.2 1.2 %reshape.10.v_ref = bf16[512,512]{1,0:T(8,128)(2,1)S(1)} reshape(bf16[256,2,512]{2,1,0:T(2,128)(2,1)} %param.9) | data formatting | bytes 1048576 | tf_op jit(solution)/shard_map/reshape | solution.py:163
  2.5 0.0 copy-start.1
  2.5 0.9 copy-done.1
  3.4 0.0 copy-start.2
  3.4 0.7 copy-done.2
  4.1 0.0 copy-start.3
  4.1 0.7 copy-done.3
  4.8 9.9 %local_terms.1 = (bf16[4,256,128]{2,1,0:T(8,128)(2,1)S(1)}, f32[4,256,128]{2,1,0:T(8,128)S(1)}, f32[4,128,128]{2,1,0:T(8,128)S(1)}, f32[4,128,128]{2,1,0:T(8,128)S(1)}) custom-call(bf16[256,512]{1,0:T(8,128)(2,1)S(1)} %copy-done.1, bf16[512,512]{1,0:T(8,128)(2,1)S(1)} %reshape.9.k_ref, bf16[512,512]{1,0:T(8,128)(2,1)S(1)} %reshape.10.v_ref, ...), custom_call_target="tpu_custom_call" | custom-call | tf_op jit(solution)/shard_map/local_terms/pallas_call | solution.py:151
  14.8 0.0 copy-start
  14.8 2.2 %copy-done = bf16[512,4096]{1,0:T(8,128)(2,1)S(1)} copy-done((bf16[512,4096]{1,0:T(8,128)(2,1)S(1)}, bf16[512,4096]{1,0:T(8,128)(2,1)}, u32[]{:S(2)}) %copy-start) | copy-done | bytes 4194328
  17.0 0.0 copy-start.4
  17.0 0.7 copy-done.4
  17.6 81.9 %finish.1 = bf16[64,4096]{1,0:T(8,128)(2,1)S(1)} custom-call(bf16[4,256,128]{2,1,0:T(8,128)(2,1)S(1)} %get-tuple-element.9.lead_ref, f32[4,256,128]{2,1,0:T(8,128)S(1)} %get-tuple-element.10.loc_ref, f32[4,128,128]{2,1,0:T(8,128)S(1)} %get-tuple-element.11.m_ref, f32[4,128,128]{2,1,0:T(8,128)S(1)} %get-tuple-element.12.o_ref, f32[1,512]{1,0:T(1,128)S(1)} %bitcast.1, ...), custom_call_target="tpu_custom_call" | custom-call | tf_op jit(solution)/shard_map/finish/pallas_call | solution.py:352
  99.6 0.8 copy.9
Async XLA Ops:
  2.5 1.0 copy-start.1
  3.4 0.7 copy-start.2
  4.1 0.7 copy-start.3
  14.8 2.2 %copy-start = (bf16[512,4096]{1,0:T(8,128)(2,1)S(1)}, bf16[512,4096]{1,0:T(8,128)(2,1)}, u32[]{:S(2)}) copy-start(bf16[512,4096]{1,0:T(8,128)(2,1)} %w_hbm.1) | copy-start | bytes 12582916
  17.0 0.7 copy-start.4

commit v3 on v2

--- a/solution.py
+++ b/solution.py
@@ -265,71 +265,68 @@
     def row_copy(p, r, to, slot):
         return remote(part.at[p, r], recv.at[p, slot], row_send_sem.at[p, r], row_recv_sem.at[p, slot], {"head": to})
 
-    def each_row(p, way):
-        for r in range(n_head):
-            @pl.when(at < r)
-            def _(r=r):
-                way(row_copy(p, r, at + 1, r))
-
-            @pl.when(at > r)
-            def _(r=r):
-                way(row_copy(p, r, at - 1, jnp.where(at - 1 == r, n_head, r)))
-
     def add(p, r, slot):
         row_copy(p, r, at, slot).wait_recv()
         part[p, r] = (part[p, r].astype(F32) + recv[p, slot].astype(F32)).astype(BF16)
 
-    def piece(p, carry):
-        @pl.when(p >= 2)
+    def sends(p, way, right):
+        for r in range(n_head):
+            @pl.when(at < r if right else at > r)
+            def _(r=r):
+                to = at + 1 if right else at - 1
+                slot = r if right else jnp.where(to == r, n_head, r)
+                way(row_copy(p, r, to, slot))
+
+    def flow(p, right):
+        @pl.when((p >= 0) & (p < pieces))
         def _():
-            each_row(p - 2, lambda copy: copy.wait_send())
-
-        columns = pl.ds(pl.multiple_of(p * width, width), width)
-        rows = mm(normed[...], weight[:, columns]).astype(BF16)
-        for r in range(n_head):
-            part[p, r] = rows[r * block : (r + 1) * block]
-        for j in range(1, n_head):
-            right, left = n_head - j, j - 1
-
-            @pl.when(at < right)
+            @pl.when(p >= 2)
             def _():
-                @pl.when(at >= 1)
-                def _():
-                    add(p, right, right)
-
-                row_copy(p, right, at + 1, right).start()
-
-            @pl.when(at > left)
-            def _():
-                @pl.when(at < n_head - 1)
-                def _():
-                    add(p, left, left)
-
-                row_copy(p, left, at - 1, jnp.where(at - 1 == left, n_head, left)).start()
+                sends(p - 2, lambda copy: copy.wait_send(), right)
+
+            for r in range(n_head - 1, 0, -1) if right else range(n_head - 1):
+                @pl.when(at < r if right else at > r)
+                def _(r=r):
+                    @pl.when(at >= 1 if right else at < n_head - 1)
+                    def _():
+                        add(p, r, r)
+
+                    to = at + 1 if right else at - 1
+                    row_copy(p, r, to, r if right else jnp.where(to == r, n_head, r)).start()
+
+    def step(i, carry):
+        @pl.when(i < pieces)
+        def _():
+            columns = pl.ds(pl.multiple_of(i * width, width), width)
+            rows = mm(normed[...], weight[:, columns]).astype(BF16)
+            for r in range(n_head):
+                part[i, r] = rows[r * block : (r + 1) * block]
+
+        flow(i - at, True)
+        flow(i - (n_head - 1 - at), False)
+        p = i - n_head
+
+        @pl.when(p >= 0)
+        def _():
+            columns = pl.ds(pl.multiple_of(p * width, width), width)
+            for r in range(n_head):
+                @pl.when(at == r)
+                def _(r=r):
+                    total = part[p, r].astype(F32)
+                    if r >= 1:
+                        row_copy(p, r, at, r).wait_recv()
+                        total = total + recv[p, r].astype(F32)
+                    if r < n_head - 1:
+                        row_copy(p, r, at, n_head).wait_recv()
+                        total = total + recv[p, n_head].astype(F32)
+                    out_ref[:, columns] = total.astype(BF16)
 
         return carry
 
-    lax.fori_loop(0, pieces, piece, 0)
-
-    def last(p, carry):
-        columns = pl.ds(pl.multiple_of(p * width, width), width)
-        for r in range(n_head):
-            @pl.when(at == r)
-            def _(r=r):
-                total = part[p, r].astype(F32)
-                if r >= 1:
-                    row_copy(p, r, at, r).wait_recv()
-                    total = total + recv[p, r].astype(F32)
-                if r < n_head - 1:
-                    row_copy(p, r, at, n_head).wait_recv()
-                    total = total + recv[p, n_head].astype(F32)
-                out_ref[:, columns] = total.astype(BF16)
-
-        return carry
-
-    lax.fori_loop(0, pieces, last, 0)
+    lax.fori_loop(0, pieces + n_head, step, 0)
     for p in range(max(pieces - 2, 0), pieces):
-        each_row(p, lambda copy: copy.wait_send())
+        sends(p, lambda copy: copy.wait_send(), True)
+        sends(p, lambda copy: copy.wait_send(), False)
 
     @pl.when(jnp.logical_not(odd))
     def _():
@@ -352,7 +349,7 @@
     return pl.pallas_call(
         functools.partial(finish_kernel, n_ctx, n_head),
         out_shape=jax.ShapeDtypeStruct((block, columns), BF16),
-        in_specs=[pl.BlockSpec(memory_space=pltpu.VMEM)] * 5 + [pl.BlockSpec(memory_space=pl.ANY)],
+        in_specs=[pl.BlockSpec(memory_space=pltpu.VMEM)] * 5 + [pl.BlockSpec(memory_space=pltpu.HBM)],
         out_specs=pl.BlockSpec(memory_space=pltpu.VMEM),
         scratch_shapes=[
             pltpu.VMEM((heads, DH, 2 * DH), BF16),

time: 101 us -> 73.3 us (0.73)
  Pallas kernels: 91.9 us -> 64.4 us
    pallas_call x1, Pallas kernels: 81.9 us -> 54.4 us  [finish(): pl.pallas_call(functools.partial(finish_kernel, n_ctx, n_head), out_shape...]
where the time goes in v3:
time: 73.3 us; the launch traced here: 72.9 us
  Pallas kernels  64.4 us (88%)
  local copies, waits for them, and re-layouts  8.47 us (12%)
    pallas_call x1, Pallas kernels, finish(): pl.pallas_call(functools.partial(finish_kernel, n_ctx, n_head), out_shape...  54.4 us
    pallas_call x1, Pallas kernels, local_terms(): pl.pallas_call(functools.partial(local_kernel, heads, tokens), out_shape=...  9.94 us
    unnamed x11, local copies, waits for them, and re-layouts  5.99 us

profile of v3, /device:TPU:6, one launch (start us, length us, event | category | flops | bytes accessed | tf_op | source)
XLA Modules:
  0.0 72.9 jit_solution(8471904557383762961)
XLA Ops:
  0.0 1.2 %reshape.9.k_ref = bf16[512,512]{1,0:T(8,128)(2,1)S(1)} reshape(bf16[256,2,512]{2,1,0:T(2,128)(2,1)} %param.8) | data formatting | bytes 1048576 | tf_op jit(solution)/shard_map/reshape | solution.py:163
  1.2 1.2 %reshape.10.v_ref = bf16[512,512]{1,0:T(8,128)(2,1)S(1)} reshape(bf16[256,2,512]{2,1,0:T(2,128)(2,1)} %param.9) | data formatting | bytes 1048576 | tf_op jit(solution)/shard_map/reshape | solution.py:163
  2.5 0.0 copy-start.1
  2.5 0.9 %copy-done.1 = bf16[256,512]{1,0:T(8,128)(2,1)S(1)} copy-done((bf16[256,512]{1,0:T(8,128)(2,1)S(1)}, bf16[256,512]{1,0:T(8,128)(2,1)}, u32[]{:S(2)}) %copy-start.1) | copy-done | bytes 262168
  3.4 0.0 copy-start.2
  3.4 0.7 copy-done.2
  4.1 0.0 copy-start.3
  4.1 0.7 copy-done.3
  4.8 9.9 %local_terms.1 = (bf16[4,256,128]{2,1,0:T(8,128)(2,1)S(1)}, f32[4,256,128]{2,1,0:T(8,128)S(1)}, f32[4,128,128]{2,1,0:T(8,128)S(1)}, f32[4,128,128]{2,1,0:T(8,128)S(1)}) custom-call(bf16[256,512]{1,0:T(8,128)(2,1)S(1)} %copy-done.1, bf16[512,512]{1,0:T(8,128)(2,1)S(1)} %reshape.9.k_ref, bf16[512,512]{1,0:T(8,128)(2,1)S(1)} %reshape.10.v_ref, ...), custom_call_target="tpu_custom_call" | custom-call | tf_op jit(solution)/shard_map/local_terms/pallas_call | solution.py:151
  14.8 0.0 copy-start
  14.8 2.2 %copy-done = bf16[512,4096]{1,0:T(8,128)(2,1)S(1)} copy-done((bf16[512,4096]{1,0:T(8,128)(2,1)S(1)}, bf16[512,4096]{1,0:T(8,128)(2,1)}, u32[]{:S(2)}) %copy-start) | copy-done | bytes 4194328
  17.0 0.0 copy-start.4
  17.0 0.7 copy-done.4
  17.6 54.4 %finish.1 = bf16[64,4096]{1,0:T(8,128)(2,1)S(1)} custom-call(bf16[4,256,128]{2,1,0:T(8,128)(2,1)S(1)} %get-tuple-element.9.lead_ref, f32[4,256,128]{2,1,0:T(8,128)S(1)} %get-tuple-element.10.loc_ref, f32[4,128,128]{2,1,0:T(8,128)S(1)} %get-tuple-element.11.m_ref, f32[4,128,128]{2,1,0:T(8,128)S(1)} %get-tuple-element.12.o_ref, f32[1,512]{1,0:T(1,128)S(1)} %bitcast.1, ...), custom_call_target="tpu_custom_call" | custom-call | tf_op jit(solution)/shard_map/finish/pallas_call | solution.py:349
  72.1 0.8 %copy.9 = bf16[64,4096]{1,0:T(8,128)(2,1)} copy(bf16[64,4096]{1,0:T(8,128)(2,1)S(1)} %finish.1) | data formatting | bytes 1048576
Async XLA Ops:
  2.5 1.0 %copy-start.1 = (bf16[256,512]{1,0:T(8,128)(2,1)S(1)}, bf16[256,512]{1,0:T(8,128)(2,1)}, u32[]{:S(2)}) copy-start(bf16[256,512]{1,0:T(8,128)(2,1)} %q_ref.1) | copy-start | bytes 786436
  3.4 0.7 copy-start.2
  4.1 0.7 copy-start.3
  14.8 2.2 %copy-start = (bf16[512,4096]{1,0:T(8,128)(2,1)S(1)}, bf16[512,4096]{1,0:T(8,128)(2,1)}, u32[]{:S(2)}) copy-start(bf16[512,4096]{1,0:T(8,128)(2,1)} %w_hbm.1) | copy-start | bytes 12582916
  17.0 0.7 copy-start.4

commit v4 on v3

--- a/solution.py
+++ b/solution.py
@@ -72,14 +72,15 @@
     blocks = [(h, c) for c in range(chunks) for h in range(heads)]
 
     def cut(h, c):
-        k = k_ref[c * steps : (c + 1) * steps, h * DH : (h + 1) * DH]
+        k = k_ref[c * span : (c + 1) * span, :, h * DH : (h + 1) * DH].reshape(steps, DH)
         q = q_ref[c * span : (c + 1) * span, h * DH : (h + 1) * DH]
-        v = v_ref[c * steps : (c + 1) * steps, h * DH : (h + 1) * DH]
+        v = v_ref[c * span : (c + 1) * span, :, h * DH : (h + 1) * DH].reshape(steps, DH)
         return q, k, v
 
     data = {}
+    cuts = {b: cut(*b) for b in blocks}
     for h, c in blocks:
-        q, k, v = cut(h, c)
+        q, k, v = cuts[h, c]
         inner = lax.dot_general(
             jnp.concatenate([k, q], axis=0), k, (((1,), (1,)), ((), ())), preferred_element_type=F32
         )
@@ -113,7 +114,7 @@
             d["inverse"] = d["inverse"] - mm_split(d["inverse"], d["part"])
     for h, c in blocks:
         d = data[h, c]
-        q, k, v = cut(h, c)
+        q, k, v = cuts[h, c]
         high, low = halves(d["inverse"])
         d["fresh"] = mm(jnp.concatenate([high, low], axis=1), jnp.concatenate([v, v], axis=0))
         high, low = halves(d["inverse"] * d["carry"])
@@ -124,7 +125,7 @@
     for c in range(chunks):
         for h in range(heads):
             d = data[h, c]
-            q, k, v = cut(h, c)
+            q, k, v = cuts[h, c]
             s_high, s_low = halves(state[h])
             w_high, w_low = halves(d["carried"])
             moved = mm(
@@ -156,16 +157,15 @@
             shape((heads, DH, DH), F32),
             shape((heads, DH, DH), F32),
         ),
-        in_specs=[pl.BlockSpec(memory_space=pltpu.VMEM)] * 5,
         out_specs=[pl.BlockSpec(memory_space=pltpu.VMEM)] * 4,
-        compiler_params=pltpu.CompilerParams(vmem_limit_bytes=40 * 2**20),
+        compiler_params=pltpu.CompilerParams(vmem_limit_bytes=62 * 2**20),
         name="local_terms",
-    )(queries, keys.reshape(2 * tokens, -1), values.reshape(2 * tokens, -1), beta, log_gate)
+    )(queries, keys, values, beta, log_gate)
 
 
 def finish_kernel(
     n_ctx, n_head, lead_ref, loc_ref, m_ref, o_ref, gain_ref, w_hbm, out_ref,
-    pair_send, pair_recv, joined, state_recv, state_send, normed, weight, part, recv,
+    pair_send, pair_recv, joined, offset, state_recv, state_send, normed, weight, part, recv,
     weight_sem, pair_send_sem, pair_recv_sem, state_send_sem, state_recv_sem, row_send_sem, row_recv_sem,
 ):
     heads = lead_ref.shape[0]
@@ -225,25 +225,33 @@
     def _():
         for h in range(heads):
             pair_copy(h).wait_recv()
-            high, low = halves(m_ref[h])
+
+    def send_state(h):
+        state_copy(h, 2).start()
+        state_copy(h, 1).start()
+
+    @pl.when(odd & has_next & jnp.logical_not(has_prev))
+    def _():
+        for h in range(heads):
+            first = pair_recv[h, :, DH:]
+            both = jnp.concatenate(halves(m_ref[h]), axis=1)
+            state_send[h] = (mm(both, jnp.concatenate([first, first], axis=0)) + o_ref[h]).astype(BF16)
+        for h in range(heads):
+            send_state(h)
+
+    @pl.when(odd & has_next & has_prev)
+    def _():
+        for h in range(heads):
+            both = jnp.concatenate(halves(m_ref[h]), axis=1)
             first = pair_recv[h]
-            joined[h] = mm(jnp.concatenate([high, low], axis=1), jnp.concatenate([first, first], axis=0))
-
-    @pl.when(odd & has_next)
-    def _():
-        for h in range(heads):
-            high, low = halves(joined[h, :, :DH])
-            both = jnp.concatenate([high, low], axis=1)
-            offset = joined[h, :, DH:] + o_ref[h]
-
-            @pl.when(has_prev)
-            def _():
-                state_copy(h, 2).wait_recv()
-
+            wide = mm(both, jnp.concatenate([first, first], axis=0))
+            joined[h] = jnp.concatenate(halves(wide[:, :DH]), axis=1)
+            offset[h] = wide[:, DH:] + o_ref[h]
+        for h in range(heads):
+            state_copy(h, 2).wait_recv()
             state = state_recv[h]
-            state_send[h] = (mm(both, jnp.concatenate([state, state], axis=0)) + offset).astype(BF16)
-            state_copy(h, 2).start()
-            state_copy(h, 1).start()
+            state_send[h] = (mm(joined[h], jnp.concatenate([state, state], axis=0)) + offset[h]).astype(BF16)
+            send_state(h)
 
     @pl.when(has_prev & jnp.logical_not(odd & has_next))
     def _():
@@ -354,7 +362,8 @@
         scratch_shapes=[
             pltpu.VMEM((heads, DH, 2 * DH), BF16),
             pltpu.VMEM((heads, DH, 2 * DH), BF16),
-            pltpu.VMEM((heads, DH, 2 * DH), F32),
+            pltpu.VMEM((heads, DH, 2 * DH), BF16),
+            pltpu.VMEM((heads, DH, DH), F32),
             pltpu.VMEM((heads, DH, DH), BF16),
             pltpu.VMEM((heads, DH, DH), BF16),
             pltpu.VMEM((tokens, heads * DH), BF16),
@@ -370,7 +379,7 @@
             dma((pieces, n_head + 1)),
         ],
         compiler_params=pltpu.CompilerParams(
-            collective_id=0, has_side_effects=True, vmem_limit_bytes=40 * 2**20
+            collective_id=0, has_side_effects=True, vmem_limit_bytes=60 * 2**20
         ),
         name="finish",
     )(lead, local_part, device_map, device_offset, norm_gain.reshape(1, -1), out_weight)

time: 73.3 us -> 70.5 us (0.962)
  local copies, waits for them, and re-layouts: 8.47 us -> 1.87 us
  Pallas kernels: 64.4 us -> 68.4 us
    unnamed x11 -> x1, local copies, waits for them, and re-layouts: 5.99 us -> 1.87 us
    reshape x2 -> x0, local copies, waits for them, and re-layouts: 2.48 us -> none  [the longest x1 1.24 us: local_terms(): values.reshape(2 * tokens, -1)]
    pallas_call x1, Pallas kernels: 9.94 us -> 12.3 us  [local_terms(): pl.pallas_call(functools.partial(local_kernel, heads, tokens), out_shape=...]
    pallas_call x1, Pallas kernels: 54.4 us -> 56.1 us  [finish(): pl.pallas_call(functools.partial(finish_kernel, n_ctx, n_head), out_shape...]
where the time goes in v4:
time: 70.5 us; the launch traced here: 70.3 us
  Pallas kernels  68.4 us (97%)
  local copies, waits for them, and re-layouts  1.87 us (3%)
    pallas_call x1, Pallas kernels, finish(): pl.pallas_call(functools.partial(finish_kernel, n_ctx, n_head), out_shape...  56.1 us
    pallas_call x1, Pallas kernels, local_terms(): pl.pallas_call(functools.partial(local_kernel, heads, tokens), out_shape=...  12.3 us
    unnamed x1, local copies, waits for them, and re-layouts  1.87 us

profile of v4, /device:TPU:6, one launch (start us, length us, event | category | flops | bytes accessed | tf_op | source)
XLA Modules:
  0.0 70.3 jit_solution(5433965677757390907)
XLA Ops:
  0.0 12.3 %local_terms.1 = (bf16[4,256,128]{2,1,0:T(8,128)(2,1)}, f32[4,256,128]{2,1,0:T(8,128)}, f32[4,128,128]{2,1,0:T(8,128)}, f32[4,128,128]{2,1,0:T(8,128)}) custom-call(bf16[256,512]{1,0:T(8,128)(2,1)} %q_ref.1, bf16[256,2,512]{2,1,0:T(2,128)(2,1)} %k_ref.1, bf16[256,2,512]{2,1,0:T(2,128)(2,1)} %v_ref.1, f32[4,2,256]{2,1,0:T(2,128)} %beta_ref.1, f32[4,256]{1,0:T(4,128)} %gate_ref.1), custom_call_target="tpu_custom_call" | custom-call | tf_op jit(solution)/shard_map/local_terms/pallas_call | solution.py:152
  12.3 56.1 %finish.1 = bf16[64,4096]{1,0:T(8,128)(2,1)} custom-call(bf16[4,256,128]{2,1,0:T(8,128)(2,1)} %get-tuple-element.9.lead_ref, f32[4,256,128]{2,1,0:T(8,128)} %get-tuple-element.10.loc_ref, f32[4,128,128]{2,1,0:T(8,128)} %get-tuple-element.11.m_ref, f32[4,128,128]{2,1,0:T(8,128)} %get-tuple-element.12.o_ref, f32[1,512]{1,0:T(1,128)} %bitcast.1, ...), custom_call_target="tpu_custom_call" | custom-call | tf_op jit(solution)/shard_map/finish/pallas_call | solution.py:357
  68.4 1.9 %copy.9 = bf16[64,4096]{1,0:T(8,128)(2,1)} copy(bf16[64,4096]{1,0:T(8,128)(2,1)} %finish.1) | data formatting | bytes 1048576
